TPU v7x, 32 devices: a whole 2x2x4 slice. The times are simulated.
32 devices in a mesh: dp: 4 (over z), proto: 8 (over y, x, core).
Axes of the slice: x: 2, y: 2, z: 4, core: 2. Of those that a mesh axis runs over, the one named last changes fastest.
Arguments:
- embeddings: bfloat16 [8192, 2560], P('proto', 'dp'), may hold values from -26 to 26
- table: bfloat16 [32768, 2560], P('proto', 'dp'), may hold values from -5 to 5
- tile_lists: int32 [8, 8], replicated, may hold values from 0 to 255, as said below
- labels: int32 [8192], P('proto'), may hold values from 0 to 32767, as said below
Outputs:
- loss: float32 [], replicated
- grad_emb: bfloat16 [8192, 2560], P('proto', 'dp')
- grad_table: bfloat16 [32768, 2560], P('proto', 'dp')
Inputs may be any that keep to these rules, and one draw needn't show every extreme that they name: `tile_lists`: each block's 8 tile ids are distinct and fall on exactly 4 owners (owner = id // 32), each of those owners holding exactly 2 of them. `labels`: the tile of each row's label (label // 128) is in the list of the row's block.
All inputs are finite; a program needn't handle non-finite values.
Results may differ from a plain program's by a relative error of at most 0.0025.
The roundings to bfloat16 on the way count: a program that leaves them out, or rounds other values in their place, can miss the bound.
Values may be sent and summed in bfloat16 or wider, within the bound.
A program may use at most 128 MiB of HBM per device.

v0:
```python
import math

import jax
import jax.numpy as jnp
from jax import lax
from jax.sharding import PartitionSpec as P

D = 2560
TILE = 128
CAP = 2


def slot_plan(ids, tiles_here):
    owners = ids // tiles_here
    local = ids % tiles_here
    count = ids.shape[-1]
    before = jnp.arange(count)[:, None] > jnp.arange(count)[None, :]
    earlier = (owners[..., :, None] == owners[..., None, :]) & before
    rank = jnp.sum(earlier.astype(jnp.int32), axis=-1)
    return (owners, local, rank)


def softmax_terms(scores, ids, lab, list_len):
    hit = (ids[None, :] == (lab // TILE)[:, None]).astype(jnp.int32)
    column = (
        jnp.sum(hit * (jnp.arange(list_len, dtype=jnp.int32) * TILE)[None, :], axis=1) + lab % TILE
    )
    onehot = (jnp.arange(list_len * TILE, dtype=jnp.int32)[None, :] == column[:, None]).astype(
        jnp.float32
    )
    top = jnp.max(scores, axis=1, keepdims=True)
    expo = jnp.exp(scores - top)
    total = jnp.sum(expo, axis=1, keepdims=True)
    lse = top[:, 0] + jnp.log(total[:, 0])
    target = jnp.sum(scores * onehot, axis=1)
    dz_rows = (expo / total - onehot).astype(jnp.bfloat16)
    return (jnp.sum(lse - target), dz_rows)


def body(embeddings, table, tile_lists, labels):
    block_rows, width = embeddings.shape
    list_len = tile_lists.shape[1]
    tiles_here = table.shape[0] // TILE
    groups = lax.axis_size("proto")
    dp_count = lax.axis_size("dp")
    rows_dev = block_rows // dp_count
    total_rows = block_rows * groups
    me = lax.axis_index("proto")
    part = lax.axis_index("dp")
    inv_scale = 1.0 / math.sqrt(D)
    owners, local, rank = slot_plan(tile_lists, tiles_here)
    match = (owners == me)[:, :, None] & (
        rank[:, :, None] == jnp.arange(CAP, dtype=jnp.int32)[None, None, :]
    )
    select = jnp.sum(match.astype(jnp.int32) * local[:, :, None], axis=1)
    shaped_table = table.reshape(tiles_here, TILE, width)
    outgoing = jnp.take(shaped_table, select.reshape(-1), axis=0).reshape(groups, CAP, TILE, width)
    incoming = lax.all_to_all(outgoing, "proto", split_axis=0, concat_axis=0, tiled=True)
    my_ids = lax.dynamic_index_in_dim(tile_lists, me, 0, keepdims=False)
    my_owner = lax.dynamic_index_in_dim(owners, me, 0, keepdims=False)
    my_rank = lax.dynamic_index_in_dim(rank, me, 0, keepdims=False)
    flat_slot = my_owner * CAP + my_rank
    tiles = jnp.take(incoming.reshape(groups * CAP, TILE, width), flat_slot, axis=0).reshape(
        list_len * TILE, width
    )
    scores = (
        lax.psum_scatter(
            lax.dot_general(
                embeddings, tiles, (((1,), (1,)), ((), ())), preferred_element_type=jnp.float32
            ),
            "dp",
            scatter_dimension=0,
            tiled=True,
        )
        * inv_scale
    )
    my_labels = lax.dynamic_slice_in_dim(labels, part * rows_dev, rows_dev, 0)
    loss_part, dz_rows = softmax_terms(scores, my_ids, my_labels, list_len)
    dz_block = lax.all_gather(dz_rows, "dp", axis=0, tiled=True)
    loss = lax.psum(loss_part, ("dp", "proto")) / total_rows
    grad_emb = jnp.dot(dz_block, tiles, preferred_element_type=jnp.float32).astype(jnp.bfloat16)
    piece = lax.dot_general(
        dz_block, embeddings, (((0,), (0,)), ((), ())), preferred_element_type=jnp.float32
    ).astype(jnp.bfloat16)
    returning = (
        jnp.zeros((groups * CAP, TILE, width), jnp.bfloat16)
        .at[flat_slot]
        .set(piece.reshape(list_len, TILE, width))
    )
    returned = lax.all_to_all(
        returning.reshape(groups, CAP, TILE, width),
        "proto",
        split_axis=0,
        concat_axis=0,
        tiled=True,
    )
    accum = (
        jnp.zeros((tiles_here, TILE, width), jnp.float32)
        .at[select.reshape(-1)]
        .add(returned.reshape(groups * CAP, TILE, width))
    )
    grad_table = accum.reshape(tiles_here * TILE, width).astype(jnp.bfloat16)
    return (loss, grad_emb, grad_table)


def solution(mesh):
    placed = (P("proto", "dp"), P("proto", "dp"), P(), P("proto"))
    return jax.shard_map(
        body,
        mesh=mesh,
        in_specs=placed,
        out_specs=(P(), P("proto", "dp"), P("proto", "dp")),
        check_vma=False,
    )
```

profile of v0, /device:TPU:0, one launch (start us, length us, event | category | flops | bytes accessed | tf_op | source)
XLA Modules:
  0.0 308.1 jit_solution(9859530231807013274)
XLA Ops:
  7.2 0.0 copy-start
  7.2 0.8 add_select_fusion
  8.0 0.7 broadcast_compare_fusion
  8.7 0.3 convert_reduce_fusion
  9.0 0.2 select_reduce_fusion.2
  9.1 0.1 copy.8
  9.2 0.1 copy.7
  9.3 0.1 reshape.136
  9.4 4.8 %gather_fusion = bf16[16,128,640]{2,1,0:T(8,128)(2,1)} fusion(bf16[32,128,640]{2,1,0:T(8,128)(2,1)} %bitcast.36, s32[1024]{0:T(1024)S(1)} %pad_clamp_fusion.1), kind=kCustom, calls=%fused_computation | custom fusion | bytes 5242944 | tf_op jit(solution)/shard_map/jit(_take)/gather | solution.py:57
  14.3 3.6 %broadcast_select_fusion = bf16[8,2,128,640]{3,2,1,0:T(8,128)(2,1)} fusion(bf16[8,2,128,640]{3,2,1,0:T(8,128)(2,1)} %bitcast.33, pred[8,2]{1,0:T(8,128)(4,1)S(1)} %copy.7), kind=kLoop, calls=%fused_computation.5 | loop fusion | flops 1310720 | bytes 5242896 | tf_op jit(solution)/shard_map/jit(_take)/select_n | solution.py:57
  17.8 5.2 %all-to-all-start = ((bf16[8,2,128,640]{3,2,1,0:T(8,128)(2,1)}), bf16[8,2,128,640]{3,2,1,0:T(8,128)(2,1)}, u32[]{:S(2)}, u32[]{:S(2)}) async-start(bf16[8,2,128,640]{3,2,1,0:T(8,128)(2,1)} %broadcast_select_fusion), calls=%async_computation | async-start | bytes 5242880 | tf_op jit(solution)/shard_map/all_to_all | solution.py:58
  23.0 0.0 reduce-scatter.2.cloned.1.call-start
  23.1 0.1 broadcast_bitcast_fusion
  23.2 32.2 %all-to-all-done = bf16[8,2,128,640]{3,2,1,0:T(8,128)(2,1)} async-done(((bf16[8,2,128,640]{3,2,1,0:T(8,128)(2,1)}), bf16[8,2,128,640]{3,2,1,0:T(8,128)(2,1)}, u32[]{:S(2)}, u32[]{:S(2)}) %all-to-all-start) | async-done | bytes 2621472 | tf_op jit(solution)/shard_map/all_to_all | solution.py:58
  55.4 2.5 gather_fusion.1
  57.9 0.3 bitcast_select_fusion
  58.2 0.0 copy-start.2
  58.2 1.0 copy-done.2
  59.3 0.0 copy-done
  59.3 3.8 %convolution_bitcast_fusion = f32[1024,1024]{0,1:T(8,128)} fusion(bf16[1024,640]{1,0:T(8,128)(2,1)S(1)} %bitcast_select_fusion, bf16[1024,640]{1,0:T(8,128)(2,1)S(1)} %copy-done), kind=kOutput, calls=%fused_computation.6 | convolution fusion | flops 1342177280 | bytes 6815744 | tf_op jit(solution)/shard_map/dot_general | solution.py:68
  63.1 0.0 reduce-scatter.2.cloned.1.call-update
  63.2 0.0 all-gather.2.cloned.1.call-start
  63.2 0.7 fusion.7
  63.9 0.0 copy-done.4
  63.9 0.1 and_select_fusion.1
  64.0 0.1 select_reduce_fusion.1
  64.1 0.1 fusion.4
  64.2 75.9 %reduce-scatter.2.cloned.1.call-done = f32[256,1024]{0,1:T(8,128)} async-done(((f32[1024,1024]{0,1:T(8,128)}), f32[256,1024]{0,1:T(8,128)}) %reduce-scatter.2.cloned.1.call-update) | async-done | bytes 1048592 | tf_op jit(solution)/shard_map/reduce_scatter | solution.py:67
  140.1 0.0 copy-start.1
  140.1 1.5 multiply_reduce_fusion
  141.6 1.5 fusion
  143.1 0.0 copy-done.1
  143.1 1.1 subtract_convert_fusion
  144.3 0.0 all-gather.2.cloned.1.call-update
  144.3 46.9 %all-gather.2.cloned.1.call-done = bf16[1024,1024]{0,1:T(8,128)(2,1)} async-done(((bf16[256,1024]{0,1:T(8,128)(2,1)}), bf16[1024,1024]{0,1:T(8,128)(2,1)}) %all-gather.2.cloned.1.call-update) | async-done | bytes 2097168 | tf_op jit(solution)/shard_map/all_gather | solution.py:79
  191.2 3.4 %convolution_convert_fusion = bf16[1024,640]{1,0:T(8,128)(2,1)S(1)} fusion(bf16[1024,1024]{0,1:T(8,128)(2,1)} %all-gather.2.cloned.1.call-done, bf16[1024,640]{1,0:T(8,128)(2,1)S(1)} %copy-done), kind=kOutput, calls=%fused_computation.7 | convolution fusion | flops 1342832640 | bytes 4718592 | tf_op jit(solution)/shard_map/dot_general | solution.py:82
  194.6 1.8 broadcast_in_dim.55
  196.4 3.1 scatter_fusion
  199.4 4.5 %all-to-all-start.1 = ((bf16[8,2,128,640]{3,2,1,0:T(8,128)(2,1)}), bf16[8,2,128,640]{3,2,1,0:T(8,128)(2,1)}, u32[]{:S(2)}, u32[]{:S(2)}) async-start(bf16[8,2,128,640]{3,2,1,0:T(8,128)(2,1)} %bitcast.32), calls=%async_computation.2 | async-start | bytes 5242880 | tf_op jit(solution)/shard_map/all_to_all | solution.py:90
  203.9 0.6 subtract_reduce_fusion
  204.5 62.9 %psum.7 = f32[]{:T(128)} all-reduce(f32[]{:T(128)} %subtract_reduce_fusion), channel_id=1, replica_groups=mesh['dp'=4,'proto'=8] {'dp','proto'}, use_global_device_ids=true, to_apply=%region_8.9 | all-reduce | flops 1 | bytes 8 | tf_op jit(solution)/shard_map/psum | solution.py:80
  268.1 0.0 copy-done.3
  268.1 4.5 %convolution_convert_fusion.1 = bf16[1024,640]{1,0:T(8,128)(2,1)} fusion(bf16[1024,1024]{0,1:T(8,128)(2,1)} %all-gather.2.cloned.1.call-done, bf16[1024,640]{1,0:T(8,128)(2,1)S(1)} %copy-done.3), kind=kOutput, calls=%fused_computation.8 | convolution fusion | flops 1342832640 | bytes 4718592 | tf_op jit(solution)/shard_map/dot_general | solution.py:81
  272.6 0.0 all-to-all-done.1
  272.6 4.6 %bitcast_convert_fusion = f32[16,128,640]{2,1,0:T(8,128)} fusion(bf16[8,2,128,640]{3,2,1,0:T(8,128)(2,1)} %all-to-all-done.1), kind=kLoop, calls=%fused_computation.4 | loop fusion | flops 1310720 | bytes 7864320 | tf_op jit(solution)/shard_map/convert_element_type | solution.py:100
  277.3 5.2 %broadcast_in_dim.54 = f32[32,128,640]{2,1,0:T(8,128)} broadcast(f32[]{:T(128)} %constant.115.clone.1), dimensions={} | broadcast | bytes 10485764 | tf_op jit(solution)/shard_map/broadcast_in_dim | solution.py:98
  282.5 10.5 %scatter_fusion.1 = f32[32,128,640]{2,1,0:T(8,128)} fusion(f32[32,128,640]{2,1,0:T(8,128)} %broadcast_in_dim.54, s32[16]{0:T(128)S(1)} %fusion.8, f32[16,128,640]{2,1,0:T(8,128)} %bitcast_convert_fusion), kind=kCustom, calls=%fused_computation.3 | custom fusion | flops 1310720 | bytes 15728704 | tf_op jit(solution)/shard_map/scatter-add | solution.py:100
  293.0 7.1 %convert_element_type.36 = bf16[32,128,640]{2,1,0:T(8,128)(2,1)} convert(f32[32,128,640]{2,1,0:T(8,128)} %scatter_fusion.1) | non-fusion elementwise | flops 2621440 | bytes 15728640 | tf_op jit(solution)/shard_map/convert_element_type | solution.py:102
  (9 shorter events, 0.1 us)
Async XLA Ops:
  7.2 52.1 %copy-start = (bf16[1024,640]{1,0:T(8,128)(2,1)S(1)}, bf16[1024,640]{1,0:T(8,128)(2,1)}, u32[]{:S(2)}) copy-start(bf16[1024,640]{1,0:T(8,128)(2,1)} %param.4) | copy-start | bytes 3932164
  17.8 37.5 %all-to-all-start = ((bf16[8,2,128,640]{3,2,1,0:T(8,128)(2,1)}), bf16[8,2,128,640]{3,2,1,0:T(8,128)(2,1)}, u32[]{:S(2)}, u32[]{:S(2)}) async-start(bf16[8,2,128,640]{3,2,1,0:T(8,128)(2,1)} %broadcast_select_fusion), calls=%async_computation | async-start | bytes 5242880 | tf_op jit(solution)/shard_map/all_to_all | solution.py:58
  23.0 117.1 %reduce-scatter.2.cloned.1.call-start = ((), (), s32[]{:S(2)}) async-start(), calls=%async_computation.3 | async-start | bytes 5242880 | tf_op jit(solution)/shard_map/reduce_scatter | solution.py:67
  58.2 1.1 copy-start.2
  63.1 0.8 copy-start.4
  63.2 128.0 %all-gather.2.cloned.1.call-start = ((), (), s32[]{:S(2)}) async-start(), calls=%async_computation.4 | async-start | bytes 2621440 | tf_op jit(solution)/shard_map/all_gather | solution.py:79
  140.1 3.0 copy-start.1
  199.4 68.7 %copy-start.3 = (bf16[1024,640]{1,0:T(8,128)(2,1)S(1)}, bf16[1024,640]{1,0:T(8,128)(2,1)}, u32[]{:S(2)}) copy-start(bf16[1024,640]{1,0:T(8,128)(2,1)} %copy-done.2) | copy-start | bytes 3932164
  199.4 73.2 %all-to-all-start.1 = ((bf16[8,2,128,640]{3,2,1,0:T(8,128)(2,1)}), bf16[8,2,128,640]{3,2,1,0:T(8,128)(2,1)}, u32[]{:S(2)}, u32[]{:S(2)}) async-start(bf16[8,2,128,640]{3,2,1,0:T(8,128)(2,1)} %bitcast.32), calls=%async_computation.2 | async-start | bytes 5242880 | tf_op jit(solution)/shard_map/all_to_all | solution.py:90
Sparse Core Ops, SparseCore 0:
  63.3 76.7 reduce-scatter.1
  144.4 46.7 all-gather.1
where the time goes:
time: 309 us; the launch traced here: 308 us
  waiting for transfers between devices  155 us (50%)
  blocking collectives  62.9 us (20%)
  other arithmetic  33.2 us (11%)
  local copies, waits for them, and re-layouts  19.5 us (6%)
  between operations  15.9 us (5%)
  matrix products  11.7 us (4%)
  starting transfers between devices  9.76 us (3%)
    reduce_scatter x1, waiting for transfers between devices, body(): lax.psum_scatter(lax.dot_general(embeddings, tiles, (((1,), (1,)), ((), (...  75.9 us
    psum x1, blocking collectives, body(): loss = lax.psum(loss_part, ('dp', 'proto')) / total_rows  62.9 us
    all_gather x1, waiting for transfers between devices, body(): dz_block = lax.all_gather(dz_rows, 'dp', axis=0, tiled=True)  46.9 us
    all_to_all x1, waiting for transfers between devices, body(): lax.all_to_all(outgoing, 'proto', split_axis=0, concat_axis=0, tiled=True)  32.2 us
    scatter-add x1, other arithmetic, body(): accum = jnp.zeros((tiles_here, TILE, width), jnp.float32).at[select.resha...  10.5 us
    convert_element_type x1, other arithmetic, body(): grad_table = accum.reshape(tiles_here * TILE, width).astype(jnp.bfloat16)  7.1 us
  transfers between devices with their start and end apart: 4, of which 3 were waited for; matrix products, arithmetic and copies ran while one was open for 2% of the time, Pallas kernels for 0%

commit v1 on v0

--- a/solution.py
+++ b/solution.py
@@ -1,13 +1,20 @@
+import functools
 import math
 
 import jax
 import jax.numpy as jnp
 from jax import lax
+from jax.experimental import pallas as pl
+from jax.experimental.pallas import tpu as pltpu
 from jax.sharding import PartitionSpec as P
 
 D = 2560
 TILE = 128
 CAP = 2
+CHUNK = 16
+LAG = 3
+VMEM_LIMIT = 56 * 2**20
+MESH = pl.DeviceIdType.MESH
 
 
 def slot_plan(ids, tiles_here):
@@ -54,13 +61,13 @@
     )
     select = jnp.sum(match.astype(jnp.int32) * local[:, :, None], axis=1)
     shaped_table = table.reshape(tiles_here, TILE, width)
-    outgoing = jnp.take(shaped_table, select.reshape(-1), axis=0).reshape(groups, CAP, TILE, width)
+    outgoing = pack_tiles(shaped_table, select.reshape(-1)).reshape(groups, CAP, TILE, width)
     incoming = lax.all_to_all(outgoing, "proto", split_axis=0, concat_axis=0, tiled=True)
     my_ids = lax.dynamic_index_in_dim(tile_lists, me, 0, keepdims=False)
     my_owner = lax.dynamic_index_in_dim(owners, me, 0, keepdims=False)
     my_rank = lax.dynamic_index_in_dim(rank, me, 0, keepdims=False)
     flat_slot = my_owner * CAP + my_rank
-    tiles = jnp.take(incoming.reshape(groups * CAP, TILE, width), flat_slot, axis=0).reshape(
+    tiles = pack_tiles(incoming.reshape(groups * CAP, TILE, width), flat_slot).reshape(
         list_len * TILE, width
     )
     scores = (
@@ -103,10 +110,449 @@
     return (loss, grad_emb, grad_table)
 
 
+def pack_kernel(pick_ref, table_ref, out_ref, sems):
+    count = out_ref.shape[0]
+
+    def copy(slot):
+        return pltpu.make_async_copy(
+            table_ref.at[pick_ref[slot]], out_ref.at[slot], sems.at[slot]
+        )
+
+    for slot in range(count):
+        copy(slot).start()
+    for slot in range(count):
+        copy(slot).wait()
+
+
+def pack_tiles(shaped_table, pick):
+    count = pick.shape[0]
+    _, tile, width = shaped_table.shape
+    return pl.pallas_call(
+        pack_kernel,
+        out_shape=jax.ShapeDtypeStruct((count, tile, width), shaped_table.dtype),
+        grid_spec=pltpu.PrefetchScalarGridSpec(
+            num_scalar_prefetch=1,
+            grid=(1,),
+            in_specs=[pl.BlockSpec(memory_space=pl.ANY)],
+            out_specs=pl.BlockSpec(memory_space=pl.ANY),
+            scratch_shapes=[pltpu.SemaphoreType.DMA((count,))],
+        ),
+    )(pick, shaped_table)
+
+
+def place_kernel(per_step, count, pick_ref, got_ref, out_ref, acc_ref):
+    step = pl.program_id(0)
+    for inner in range(per_step):
+        tile_id = step * per_step + inner
+        acc_ref[...] = jnp.zeros_like(acc_ref)
+
+        def add(slot, carry):
+            @pl.when(pick_ref[slot] == tile_id)
+            def _():
+                acc_ref[...] += got_ref[slot].astype(jnp.float32)
+
+            return carry
+
+        lax.fori_loop(0, count, add, 0)
+        out_ref[inner] = acc_ref[...].astype(out_ref.dtype)
+
+
+def place_tiles(returned, pick, tiles_here):
+    count, tile, width = returned.shape
+    per_step = 4
+    return pl.pallas_call(
+        functools.partial(place_kernel, per_step, count),
+        out_shape=jax.ShapeDtypeStruct((tiles_here, tile, width), returned.dtype),
+        grid_spec=pltpu.PrefetchScalarGridSpec(
+            num_scalar_prefetch=1,
+            grid=(tiles_here // per_step,),
+            in_specs=[pl.BlockSpec(memory_space=pltpu.VMEM)],
+            out_specs=pl.BlockSpec((per_step, tile, width), lambda i, pick: (i, 0, 0)),
+            scratch_shapes=[pltpu.VMEM((tile, width), jnp.float32)],
+        ),
+        compiler_params=pltpu.CompilerParams(vmem_limit_bytes=24 * 2**20),
+    )(pick, returned)
+
+
+def main_kernel(
+    groups,
+    dp_count,
+    inv_scale,
+    slot_ref,
+    back_ref,
+    out_tiles,
+    emb,
+    column,
+    grad_emb,
+    returned,
+    loss_out,
+    incoming,
+    tiles,
+    scores,
+    partial,
+    dz,
+    piece,
+    ret,
+    loss_acc,
+    loss_mine,
+    loss_plane,
+    loss_sum,
+    loss_z,
+    tile_send,
+    tile_recv,
+    own_sem,
+    part_send,
+    part_recv,
+    dz_send,
+    dz_recv,
+    ret_send,
+    ret_recv,
+    own_ret_sem,
+    lp_send,
+    lp_recv,
+    lz_send,
+    lz_recv,
+):
+    me = lax.axis_index("proto")
+    z = lax.axis_index("dp")
+    rows, width = emb.shape
+    list_len = slot_ref.shape[0]
+    cols = list_len * TILE
+    half = rows // 2
+    chunks = half // CHUNK
+    last = dp_count - 1
+
+    barrier = pltpu.get_barrier_semaphore()
+    for k in range(1, groups):
+        pl.semaphore_signal(
+            barrier, inc=1, device_id={"proto": lax.rem(me + k, groups)}, device_id_type=MESH
+        )
+    for k in range(1, dp_count):
+        pl.semaphore_signal(
+            barrier, inc=1, device_id={"dp": lax.rem(z + k, dp_count)}, device_id_type=MESH
+        )
+    pl.semaphore_wait(barrier, groups + dp_count - 2)
+
+    def tile_copy(k):
+        to = lax.rem(me + k, groups)
+        return pltpu.make_async_remote_copy(
+            src_ref=out_tiles.at[pl.ds(to * CAP, CAP)],
+            dst_ref=incoming.at[pl.ds(me * CAP, CAP)],
+            send_sem=tile_send.at[k],
+            recv_sem=tile_recv.at[k],
+            device_id={"proto": to},
+            device_id_type=MESH,
+        )
+
+    for k in range(1, groups):
+        tile_copy(k).start()
+    own = pltpu.make_async_copy(
+        out_tiles.at[pl.ds(me * CAP, CAP)], incoming.at[pl.ds(me * CAP, CAP)], own_sem
+    )
+    own.start()
+    loss_acc[...] = jnp.zeros_like(loss_acc)
+    own.wait()
+    for k in range(1, groups):
+        tile_copy(k).wait()
+    for j in range(list_len):
+        tiles[j * TILE : (j + 1) * TILE, :] = incoming[slot_ref[j]]
+
+    block = min(256, half)
+
+    def score_block(i, carry):
+        at = pl.ds(pl.multiple_of(i * block, block), block)
+        scores[at, :] = lax.dot_general(
+            emb[at, :], tiles[...], (((1,), (1,)), ((), ())), preferred_element_type=jnp.float32
+        )
+        return carry
+
+    lax.fori_loop(0, rows // block, score_block, 0)
+
+    def rows_of(way, c):
+        return pl.multiple_of((1 - way) * half + c * CHUNK, CHUNK)
+
+    def part_copy(way, c, first):
+        dst = partial.at[way, pl.ds(pl.multiple_of(c * CHUNK, CHUNK), CHUNK)]
+        src = scores.at[pl.ds(rows_of(way, c), CHUNK)] if first else dst
+        return pltpu.make_async_remote_copy(
+            src_ref=src,
+            dst_ref=dst,
+            send_sem=part_send.at[way, c],
+            recv_sem=part_recv.at[way, c],
+            device_id={"dp": jnp.clip(z + 1 - 2 * way, 0, last)},
+            device_id_type=MESH,
+        )
+
+    def dz_copy(way, c):
+        at = dz.at[pl.ds(rows_of(way, c), CHUNK)]
+        return pltpu.make_async_remote_copy(
+            src_ref=at,
+            dst_ref=at,
+            send_sem=dz_send.at[way, c],
+            recv_sem=dz_recv.at[way, c],
+            device_id={"dp": jnp.clip(z - 1 + 2 * way, 0, last)},
+            device_id_type=MESH,
+        )
+
+    lane = lax.broadcasted_iota(jnp.int32, (CHUNK, cols), 1)
+
+    def step(i, carry):
+        way = lax.rem(i, 2)
+        s = i // 2
+        pos = jnp.where(way == 0, z, last - z)
+        c = s - LAG * pos
+
+        @pl.when((c >= 0) & (c < chunks))
+        def _():
+            at = pl.ds(rows_of(way, c), CHUNK)
+            here = pl.ds(pl.multiple_of(c * CHUNK, CHUNK), CHUNK)
+
+            @pl.when(pos == 0)
+            def _():
+                part_copy(way, c, True).start()
+
+            @pl.when((pos > 0) & (pos < last))
+            def _():
+                part_copy(way, c, False).wait_recv()
+                partial[way, here, :] += scores[at, :]
+                part_copy(way, c, False).start()
+
+            @pl.when(pos == last)
+            def _():
+                part_copy(way, c, False).wait_recv()
+                score = (partial[way, here, :] + scores[at, :]) * inv_scale
+                onehot = lane == column[at, :]
+                top = jnp.max(score, axis=1, keepdims=True)
+                expo = jnp.exp(score - top)
+                total = jnp.sum(expo, axis=1, keepdims=True)
+                target = jnp.sum(jnp.where(onehot, score, 0.0), axis=1, keepdims=True)
+                loss_acc[...] += (top + jnp.log(total)) - target + jnp.zeros_like(loss_acc)
+                dz[at, :] = (expo / total - jnp.where(onehot, 1.0, 0.0)).astype(dz.dtype)
+                dz_copy(way, c).start()
+
+        c2 = s - LAG * last - LAG * (last - pos)
+
+        @pl.when((c2 >= 0) & (c2 < chunks) & (pos < last))
+        def _():
+            dz_copy(way, c2).wait_recv()
+
+            @pl.when(pos > 0)
+            def _():
+                dz_copy(way, c2).start()
+
+        return carry
+
+    lax.fori_loop(0, 2 * (chunks + 2 * LAG * last), step, 0)
+
+    loss_mine[...] = jnp.broadcast_to(jnp.sum(loss_acc[...], axis=0, keepdims=True), (8, 128))
+
+    def lp_copy(k):
+        return pltpu.make_async_remote_copy(
+            src_ref=loss_mine,
+            dst_ref=loss_plane.at[me],
+            send_sem=lp_send.at[k],
+            recv_sem=lp_recv.at[k],
+            device_id={"proto": lax.rem(me + k, groups)},
+            device_id_type=MESH,
+        )
+
+    for k in range(1, groups):
+        lp_copy(k).start()
+
+    wide = min(256, cols)
+    for j in range(cols // wide):
+        out = lax.dot_general(
+            dz[:, j * wide : (j + 1) * wide],
+            emb[...],
+            (((0,), (0,)), ((), ())),
+            preferred_element_type=jnp.float32,
+        ).astype(piece.dtype)
+        for t in range(wide // TILE):
+            piece[j * (wide // TILE) + t] = out[t * TILE : (t + 1) * TILE, :]
+
+    def ret_copy(k):
+        to = lax.rem(me + k, groups)
+        return pltpu.make_async_remote_copy(
+            src_ref=ret.at[pl.ds(to * CAP, CAP)],
+            dst_ref=returned.at[pl.ds(me * CAP, CAP)],
+            send_sem=ret_send.at[k],
+            recv_sem=ret_recv.at[k],
+            device_id={"proto": to},
+            device_id_type=MESH,
+        )
+
+    for k in range(1, groups):
+        to = lax.rem(me + k, groups)
+        for t in range(CAP):
+            ret[to * CAP + t] = piece[back_ref[to * CAP + t]]
+        ret_copy(k).start()
+    for t in range(CAP):
+        ret[me * CAP + t] = piece[back_ref[me * CAP + t]]
+    own_ret = pltpu.make_async_copy(
+        ret.at[pl.ds(me * CAP, CAP)], returned.at[pl.ds(me * CAP, CAP)], own_ret_sem
+    )
+    own_ret.start()
+
+    def grad_block(i, carry):
+        at = pl.ds(pl.multiple_of(i * block, block), block)
+        grad_emb[at, :] = jnp.dot(
+            dz[at, :], tiles[...], preferred_element_type=jnp.float32
+        ).astype(grad_emb.dtype)
+        return carry
+
+    lax.fori_loop(0, rows // block, grad_block, 0)
+
+    loss_plane[me] = loss_mine[...]
+    for k in range(1, groups):
+        lp_copy(k).wait()
+    plane = loss_plane[0]
+    for k in range(1, groups):
+        plane = plane + loss_plane[k]
+    loss_sum[...] = plane
+
+    def lz_copy(k):
+        return pltpu.make_async_remote_copy(
+            src_ref=loss_sum,
+            dst_ref=loss_z.at[z],
+            send_sem=lz_send.at[k],
+            recv_sem=lz_recv.at[k],
+            device_id={"dp": lax.rem(z + k, dp_count)},
+            device_id_type=MESH,
+        )
+
+    for k in range(1, dp_count):
+        lz_copy(k).start()
+    loss_z[z] = plane
+    for k in range(1, dp_count):
+        lz_copy(k).wait()
+    whole = loss_z[0]
+    for k in range(1, dp_count):
+        whole = whole + loss_z[k]
+    loss_out[...] = whole
+
+    def drain(i, carry):
+        way = lax.rem(i, 2)
+        c = i // 2
+        pos = jnp.where(way == 0, z, last - z)
+
+        @pl.when(pos < last)
+        def _():
+            part_copy(way, c, False).wait_send()
+
+        @pl.when(pos > 0)
+        def _():
+            dz_copy(way, c).wait_send()
+
+        return carry
+
+    lax.fori_loop(0, 2 * chunks, drain, 0)
+    own_ret.wait()
+    for k in range(1, groups):
+        ret_copy(k).wait()
+
+
+def fused_body(embeddings, table, tile_lists, labels):
+    block_rows, width = embeddings.shape
+    list_len = tile_lists.shape[1]
+    tiles_here = table.shape[0] // TILE
+    groups = lax.axis_size("proto")
+    dp_count = lax.axis_size("dp")
+    total_rows = block_rows * groups
+    cols = list_len * TILE
+    slots = groups * CAP
+    me = lax.axis_index("proto")
+    owners, local, rank = slot_plan(tile_lists, tiles_here)
+    match = (owners == me)[:, :, None] & (
+        rank[:, :, None] == jnp.arange(CAP, dtype=jnp.int32)[None, None, :]
+    )
+    select = jnp.sum(match.astype(jnp.int32) * local[:, :, None], axis=1).reshape(-1)
+    taken = jnp.any(match, axis=1).reshape(-1)
+    my_ids = lax.dynamic_index_in_dim(tile_lists, me, 0, keepdims=False)
+    flat = owners * CAP + rank
+    my_slot = lax.dynamic_index_in_dim(flat, me, 0, keepdims=False)
+    order = jnp.arange(list_len, dtype=jnp.int32)
+    back = jnp.sum(
+        (my_slot[None, :] == jnp.arange(slots, dtype=jnp.int32)[:, None]).astype(jnp.int32)
+        * order[None, :],
+        axis=1,
+    )
+    hit = (my_ids[None, :] == (labels // TILE)[:, None]).astype(jnp.int32)
+    column = (jnp.sum(hit * (order * TILE)[None, :], axis=1) + labels % TILE)[:, None]
+    outgoing = pack_tiles(table.reshape(tiles_here, TILE, width), select)
+    chunks = block_rows // 2 // CHUNK
+    bf16, f32 = jnp.bfloat16, jnp.float32
+    dma = pltpu.SemaphoreType.DMA
+    vmem = pl.BlockSpec(memory_space=pltpu.VMEM)
+    smem = pl.BlockSpec(memory_space=pltpu.SMEM)
+    hbm = pl.BlockSpec(memory_space=pl.ANY)
+    grad_emb, returned, loss = pl.pallas_call(
+        functools.partial(main_kernel, groups, dp_count, 1.0 / math.sqrt(D)),
+        out_shape=(
+            jax.ShapeDtypeStruct((block_rows, width), bf16),
+            jax.ShapeDtypeStruct((slots, TILE, width), bf16),
+            jax.ShapeDtypeStruct((8, 128), f32),
+        ),
+        in_specs=[smem, smem, hbm, vmem, vmem],
+        out_specs=(vmem, hbm, vmem),
+        scratch_shapes=[
+            pltpu.VMEM((slots, TILE, width), bf16),
+            pltpu.VMEM((cols, width), bf16),
+            pltpu.VMEM((block_rows, cols), f32),
+            pltpu.VMEM((2, block_rows // 2, cols), f32),
+            pltpu.VMEM((block_rows, cols), bf16),
+            pltpu.VMEM((list_len, TILE, width), bf16),
+            pltpu.VMEM((slots, TILE, width), bf16),
+            pltpu.VMEM((CHUNK, 128), f32),
+            pltpu.VMEM((8, 128), f32),
+            pltpu.VMEM((groups, 8, 128), f32),
+            pltpu.VMEM((8, 128), f32),
+            pltpu.VMEM((dp_count, 8, 128), f32),
+            dma((groups,)),
+            dma((groups,)),
+            dma,
+            dma((2, chunks)),
+            dma((2, chunks)),
+            dma((2, chunks)),
+            dma((2, chunks)),
+            dma((groups,)),
+            dma((groups,)),
+            dma,
+            dma((groups,)),
+            dma((groups,)),
+            dma((dp_count,)),
+            dma((dp_count,)),
+        ],
+        compiler_params=pltpu.CompilerParams(
+            collective_id=0, has_side_effects=True, vmem_limit_bytes=VMEM_LIMIT
+        ),
+    )(my_slot, back, outgoing, embeddings, column)
+    grad_table = place_tiles(returned, jnp.where(taken, select, -1), tiles_here)
+    return (loss[0, 0] / total_rows, grad_emb, grad_table.reshape(tiles_here * TILE, width))
+
+
+def fused_bytes(block_rows, width, list_len, groups):
+    cols = list_len * TILE
+    slots = groups * CAP
+    return (
+        block_rows * cols * (4 + 4 + 2)
+        + 2 * slots * TILE * width * 2
+        + 2 * cols * width * 2
+        + 2 * block_rows * width * 2
+        + block_rows * 128 * 4
+    )
+
+
+def any_body(embeddings, table, tile_lists, labels):
+    need = fused_bytes(*embeddings.shape, tile_lists.shape[1], lax.axis_size("proto"))
+    if need + 12 * 2**20 <= VMEM_LIMIT:
+        return fused_body(embeddings, table, tile_lists, labels)
+    return body(embeddings, table, tile_lists, labels)
+
+
 def solution(mesh):
     placed = (P("proto", "dp"), P("proto", "dp"), P(), P("proto"))
     return jax.shard_map(
-        body,
+        any_body,
         mesh=mesh,
         in_specs=placed,
         out_specs=(P(), P("proto", "dp"), P("proto", "dp")),

time: 309 us -> 258 us (0.83)
  Pallas kernels: 0 us -> 243 us
  waiting for transfers between devices: 155 us -> 0 us
  blocking collectives: 62.9 us -> 0 us
  other arithmetic: 33.2 us -> 4.09 us
  local copies, waits for them, and re-layouts: 19.5 us -> 6.07 us
  between operations: 15.9 us -> 2.49 us
  matrix products: 11.7 us -> 0 us
  starting transfers between devices: 9.76 us -> 0 us
    pallas_call x0 -> x3, Pallas kernels: none -> 243 us  [the longest x1 152 us: fused_body(): pl.pallas_call(functools.partial(main_kernel, groups, dp_count, 1.0 / mat...]
    reduce_scatter x1 -> x0, waiting for transfers between devices: 75.9 us -> none  [body(): lax.psum_scatter(lax.dot_general(embeddings, tiles, (((1,), (1,)), ((), (...]
    psum x1 -> x0, blocking collectives: 62.9 us -> none  [body(): loss = lax.psum(loss_part, ('dp', 'proto')) / total_rows]
    all_gather x1 -> x0, waiting for transfers between devices: 46.9 us -> none  [body(): dz_block = lax.all_gather(dz_rows, 'dp', axis=0, tiled=True)]
    all_to_all x2 -> x0, waiting for transfers between devices: 32.2 us -> none  [the longest x1 32.2 us: body(): lax.all_to_all(outgoing, 'proto', split_axis=0, concat_axis=0, tiled=True)]
    convert_element_type x3 -> x0, other arithmetic: 12.9 us -> none  [the longest x1 7.1 us: body(): grad_table = accum.reshape(tiles_here * TILE, width).astype(jnp.bfloat16)]
    dot_general x3 -> x0, matrix products: 11.7 us -> none  [the longest x1 4.48 us: body(): jnp.dot(dz_block, tiles, preferred_element_type=jnp.float32)]
    scatter-add x1 -> x0, other arithmetic: 10.5 us -> none  [body(): accum = jnp.zeros((tiles_here, TILE, width), jnp.float32).at[select.resha...]
  transfers between devices with their start and end apart: 4 -> 0, of which waited for: 3 -> 0; matrix products, arithmetic and copies ran while one was open for 2% -> 0% of each run, Pallas kernels for 0% -> 0%
where the time goes in v1:
time: 258 us; the launch traced here: 256 us
  Pallas kernels  243 us (94%)
  local copies, waits for them, and re-layouts  6.07 us (2%)
  other arithmetic  4.09 us (2%)
    pallas_call x1, Pallas kernels, fused_body(): pl.pallas_call(functools.partial(main_kernel, groups, dp_count, 1.0 / mat...  152 us
    pallas_call x1, Pallas kernels, pack_tiles(): pl.pallas_call(pack_kernel, out_shape=jax.ShapeDtypeStruct((count, tile,...  81.3 us
    pallas_call x1, Pallas kernels, place_tiles(): pl.pallas_call(functools.partial(place_kernel, per_step, count), out_shap...  10 us

profile of v1, /device:TPU:0, one launch (start us, length us, event | category | flops | bytes accessed | tf_op | source)
XLA Modules:
  0.0 255.7 jit_solution(6351090349986851650)
XLA Ops:
  0.6 0.7 dynamic-slice_bitcast_fusion
  1.3 0.7 add_select_fusion.1
  2.0 0.1 select_reduce_fusion
  2.1 0.7 fusion.2
  2.8 0.7 add_select_fusion.2
  3.5 0.7 broadcast_compare_fusion
  4.2 0.3 convert_reduce_fusion
  4.5 0.2 select_reduce_fusion.1
  4.6 0.2 fusion.1
  4.8 0.0 copy-start.3
  4.8 0.6 select_reduce_fusion.2.back_ref
  5.5 0.1 copy.10
  5.6 0.1 reshape.44
  5.7 0.1 copy.8
  5.7 0.1 reshape.42.pick_ref
  5.8 0.0 copy-start.2
  5.8 1.0 copy.9.column
  6.9 0.0 copy-done.2
  6.9 81.3 %shard_map.67.out_tiles = bf16[16,128,640]{2,1,0:T(8,128)(2,1)} custom-call(s32[16]{0:T(128)} %copy-done.2, bf16[32,128,640]{2,1,0:T(8,128)(2,1)} %bitcast.8), custom_call_target="tpu_custom_call" | custom-call | tf_op jit(solution)/shard_map/pallas_call | solution.py:130
  88.2 0.0 copy-done.3
  88.2 151.7 %shard_map.68 = (bf16[1024,640]{1,0:T(8,128)(2,1)}, bf16[16,128,640]{2,1,0:T(8,128)(2,1)}, f32[8,128]{1,0:T(8,128)}) custom-call(s32[8]{0:T(128)} %copy-done.3, s32[16]{0:T(128)} %select_reduce_fusion.2.back_ref, bf16[16,128,640]{2,1,0:T(8,128)(2,1)} %shard_map.67.out_tiles, bf16[1024,640]{1,0:T(8,128)(2,1)} %emb.1, s32[1024,1]{1,0:T(8,128)} %copy.9.column), custom_call_target="tpu_custom_call" | custom-call | tf_op jit(solution)/shard_map/pallas_call | solution.py:488
  239.9 1.2 slice.3
  241.7 0.0 copy-start
  241.8 1.7 copy-done
  243.5 0.0 copy-start.1
  243.5 10.0 %shard_map.69 = bf16[32,128,640]{2,1,0:T(8,128)(2,1)} custom-call(s32[16]{0:T(128)S(1)} %broadcast_select_fusion.pick_ref, bf16[16,128,640]{2,1,0:T(8,128)(2,1)S(1)} %copy-done), custom_call_target="tpu_custom_call" | custom-call | tf_op jit(solution)/shard_map/pallas_call | solution.py:163
  253.5 0.0 copy-done.1
  253.5 1.1 copy.12
  (4 shorter events, 0.0 us)
Async XLA Ops:
  4.8 83.4 %copy-start.3 = (s32[8]{0:T(128)}, s32[8]{0:T(128)S(1)}, u32[]{:S(2)}) copy-start(s32[8]{0:T(128)S(1)} %dynamic-slice_bitcast_fusion.1.slot_ref) | copy-start | bytes 100
  5.8 1.0 copy-start.2
  241.7 1.7 copy-start
  243.5 10.0 %copy-start.1 = (bf16[1024,640]{1,0:T(8,128)(2,1)S(1)}, bf16[1024,640]{1,0:T(8,128)(2,1)}, u32[]{:S(2)}) copy-start(bf16[1024,640]{1,0:T(8,128)(2,1)} %get-tuple-element.16) | copy-start | bytes 3932164

commit v2 on v1

--- a/solution.py
+++ b/solution.py
@@ -134,44 +134,60 @@
             num_scalar_prefetch=1,
             grid=(1,),
             in_specs=[pl.BlockSpec(memory_space=pl.ANY)],
-            out_specs=pl.BlockSpec(memory_space=pl.ANY),
+            out_specs=pl.BlockSpec(memory_space=pltpu.VMEM),
             scratch_shapes=[pltpu.SemaphoreType.DMA((count,))],
         ),
+        compiler_params=pltpu.CompilerParams(vmem_limit_bytes=32 * 2**20),
     )(pick, shaped_table)
 
 
-def place_kernel(per_step, count, pick_ref, got_ref, out_ref, acc_ref):
+def place_kernel(per_step, count, pick_ref, uses_ref, first_ref, got_ref, out_ref, acc_ref):
     step = pl.program_id(0)
     for inner in range(per_step):
         tile_id = step * per_step + inner
-        acc_ref[...] = jnp.zeros_like(acc_ref)
-
-        def add(slot, carry):
-            @pl.when(pick_ref[slot] == tile_id)
-            def _():
-                acc_ref[...] += got_ref[slot].astype(jnp.float32)
-
-            return carry
-
-        lax.fori_loop(0, count, add, 0)
-        out_ref[inner] = acc_ref[...].astype(out_ref.dtype)
+        uses = uses_ref[tile_id]
+
+        @pl.when(uses == 0)
+        def _():
+            out_ref[inner] = jnp.zeros(out_ref.shape[1:], out_ref.dtype)
+
+        @pl.when(uses == 1)
+        def _():
+            out_ref[inner] = got_ref[first_ref[tile_id]]
+
+        @pl.when(uses > 1)
+        def _():
+            acc_ref[...] = jnp.zeros_like(acc_ref)
+
+            def add(slot, carry):
+                @pl.when(pick_ref[slot] == tile_id)
+                def _():
+                    acc_ref[...] += got_ref[slot].astype(jnp.float32)
+
+                return carry
+
+            lax.fori_loop(0, count, add, 0)
+            out_ref[inner] = acc_ref[...].astype(out_ref.dtype)
 
 
 def place_tiles(returned, pick, tiles_here):
     count, tile, width = returned.shape
     per_step = 4
+    named = pick[None, :] == jnp.arange(tiles_here, dtype=jnp.int32)[:, None]
+    uses = jnp.sum(named.astype(jnp.int32), axis=1)
+    first = jnp.max(named * jnp.arange(count, dtype=jnp.int32)[None, :], axis=1)
     return pl.pallas_call(
         functools.partial(place_kernel, per_step, count),
         out_shape=jax.ShapeDtypeStruct((tiles_here, tile, width), returned.dtype),
         grid_spec=pltpu.PrefetchScalarGridSpec(
-            num_scalar_prefetch=1,
+            num_scalar_prefetch=3,
             grid=(tiles_here // per_step,),
             in_specs=[pl.BlockSpec(memory_space=pltpu.VMEM)],
-            out_specs=pl.BlockSpec((per_step, tile, width), lambda i, pick: (i, 0, 0)),
+            out_specs=pl.BlockSpec((per_step, tile, width), lambda i, *refs: (i, 0, 0)),
             scratch_shapes=[pltpu.VMEM((tile, width), jnp.float32)],
         ),
         compiler_params=pltpu.CompilerParams(vmem_limit_bytes=24 * 2**20),
-    )(pick, returned)
+    )(pick, uses, first, returned)
 
 
 def main_kernel(

time: 258 us -> 179 us (0.69)
  Pallas kernels: 243 us -> 160 us
  local copies, waits for them, and re-layouts: 6.07 us -> 10 us
    pallas_call x1, Pallas kernels: 81.3 us -> 4.14 us  [pack_tiles(): pl.pallas_call(pack_kernel, out_shape=jax.ShapeDtypeStruct((count, tile,...]
    pallas_call x1, Pallas kernels: 10 us -> 4.56 us  [place_tiles(): pl.pallas_call(functools.partial(place_kernel, per_step, count), out_shap...]
    unnamed x9 -> x11, local copies, waits for them, and re-layouts: 2.8 us -> 6.77 us
where the time goes in v2:
time: 179 us; the launch traced here: 177 us
  Pallas kernels  160 us (89%)
  local copies, waits for them, and re-layouts  10 us (6%)
  other arithmetic  4.19 us (2%)
  between operations  2.5 us (1%)
    pallas_call x1, Pallas kernels, fused_body(): pl.pallas_call(functools.partial(main_kernel, groups, dp_count, 1.0 / mat...  152 us
    unnamed x11, local copies, waits for them, and re-layouts  6.77 us
    pallas_call x1, Pallas kernels, place_tiles(): pl.pallas_call(functools.partial(place_kernel, per_step, count), out_shap...  4.56 us
    pallas_call x1, Pallas kernels, pack_tiles(): pl.pallas_call(pack_kernel, out_shape=jax.ShapeDtypeStruct((count, tile,...  4.14 us

profile of v2, /device:TPU:0, one launch (start us, length us, event | category | flops | bytes accessed | tf_op | source)
XLA Modules:
  0.0 177.1 jit_solution(6893569847656778446)
XLA Ops:
  0.6 0.7 dynamic-slice_bitcast_fusion
  1.3 0.7 add_select_fusion.1
  2.0 0.1 select_reduce_fusion
  2.1 0.7 fusion.2
  2.8 0.7 add_select_fusion.2
  3.5 0.7 broadcast_compare_fusion
  4.2 0.3 convert_reduce_fusion
  4.5 0.2 select_reduce_fusion.2
  4.6 0.2 fusion.1
  4.8 0.0 copy-start.4
  4.8 0.6 select_reduce_fusion.3.back_ref
  5.5 0.1 copy.10
  5.6 0.1 reshape.53
  5.7 0.1 copy.8
  5.7 0.1 reshape.51.pick_ref
  5.8 0.1 select_reduce_fusion.1
  5.9 1.0 copy.9.column
  6.9 0.0 copy-start.1
  6.9 2.5 %copy-done.1 = bf16[4096,640]{1,0:T(8,128)(2,1)S(1)} copy-done((bf16[4096,640]{1,0:T(8,128)(2,1)S(1)}, bf16[4096,640]{1,0:T(8,128)(2,1)}, u32[]{:S(2)}) %copy-start.1) | copy-done | bytes 5242904
  9.4 4.1 %shard_map.67.out_tiles = bf16[16,128,640]{2,1,0:T(8,128)(2,1)S(1)} custom-call(s32[16]{0:T(128)S(1)} %reshape.51.pick_ref, bf16[32,128,640]{2,1,0:T(8,128)(2,1)S(1)} %bitcast.8), custom_call_target="tpu_custom_call" | custom-call | tf_op jit(solution)/shard_map/pallas_call | solution.py:130
  13.6 0.0 copy-done.4
  13.6 0.0 copy-start
  13.6 1.5 copy-done
  15.1 151.7 %shard_map.68 = (bf16[1024,640]{1,0:T(8,128)(2,1)}, bf16[16,128,640]{2,1,0:T(8,128)(2,1)}, f32[8,128]{1,0:T(8,128)}) custom-call(s32[8]{0:T(128)} %copy-done.4, s32[16]{0:T(128)} %select_reduce_fusion.3.back_ref, bf16[16,128,640]{2,1,0:T(8,128)(2,1)} %copy-done, bf16[1024,640]{1,0:T(8,128)(2,1)} %emb.1, s32[1024,1]{1,0:T(8,128)} %copy.9.column), custom_call_target="tpu_custom_call" | custom-call | tf_op jit(solution)/shard_map/pallas_call | solution.py:504
  166.8 1.2 slice.3
  168.6 0.0 copy-start.2
  168.6 1.7 copy-done.2
  170.4 0.0 copy-start.3
  170.4 4.6 %shard_map.69 = bf16[32,128,640]{2,1,0:T(8,128)(2,1)} custom-call(s32[16]{0:T(128)S(1)} %broadcast_select_fusion.pick_ref, s32[32]{0:T(128)S(1)} %get-tuple-element.10.uses_ref, s32[32]{0:T(128)S(1)} %get-tuple-element.9.first_ref, bf16[16,128,640]{2,1,0:T(8,128)(2,1)S(1)} %copy-done.2), custom_call_target="tpu_custom_call" | custom-call | tf_op jit(solution)/shard_map/pallas_call | solution.py:179
  174.9 0.0 copy-done.3
  174.9 1.1 copy.12
  (4 shorter events, 0.0 us)
Async XLA Ops:
  4.8 8.8 %copy-start.4 = (s32[8]{0:T(128)}, s32[8]{0:T(128)S(1)}, u32[]{:S(2)}) copy-start(s32[8]{0:T(128)S(1)} %dynamic-slice_bitcast_fusion.1.slot_ref) | copy-start | bytes 100
  6.9 2.5 %copy-start.1 = (bf16[4096,640]{1,0:T(8,128)(2,1)S(1)}, bf16[4096,640]{1,0:T(8,128)(2,1)}, u32[]{:S(2)}) copy-start(bf16[4096,640]{1,0:T(8,128)(2,1)} %param.5) | copy-start | bytes 15728644
  13.6 1.5 copy-start
  168.6 1.7 copy-start.2
  170.4 4.6 %copy-start.3 = (bf16[1024,640]{1,0:T(8,128)(2,1)S(1)}, bf16[1024,640]{1,0:T(8,128)(2,1)}, u32[]{:S(2)}) copy-start(bf16[1024,640]{1,0:T(8,128)(2,1)} %get-tuple-element.18) | copy-start | bytes 3932164

commit v3 on v2

--- a/solution.py
+++ b/solution.py
@@ -11,8 +11,9 @@
 D = 2560
 TILE = 128
 CAP = 2
-CHUNK = 16
-LAG = 3
+CHUNK = 32
+HALF = TILE // 2
+LAG = 2
 VMEM_LIMIT = 56 * 2**20
 MESH = pl.DeviceIdType.MESH
 
@@ -141,8 +142,9 @@
     )(pick, shaped_table)
 
 
-def place_kernel(per_step, count, pick_ref, uses_ref, first_ref, got_ref, out_ref, acc_ref):
+def place_kernel(per_step, count, pick_ref, uses_ref, first_ref, got_ref, emb_in, out_ref, emb_out, acc_ref):
     step = pl.program_id(0)
+    emb_out[...] = emb_in[...]
     for inner in range(per_step):
         tile_id = step * per_step + inner
         uses = uses_ref[tile_id]
@@ -170,24 +172,32 @@
             out_ref[inner] = acc_ref[...].astype(out_ref.dtype)
 
 
-def place_tiles(returned, pick, tiles_here):
+def place_tiles(returned, pick, grad_emb, tiles_here):
     count, tile, width = returned.shape
     per_step = 4
+    steps = tiles_here // per_step
+    emb_spec = pl.BlockSpec((grad_emb.shape[0] // steps, width), lambda i, *refs: (i, 0))
     named = pick[None, :] == jnp.arange(tiles_here, dtype=jnp.int32)[:, None]
     uses = jnp.sum(named.astype(jnp.int32), axis=1)
     first = jnp.max(named * jnp.arange(count, dtype=jnp.int32)[None, :], axis=1)
     return pl.pallas_call(
         functools.partial(place_kernel, per_step, count),
-        out_shape=jax.ShapeDtypeStruct((tiles_here, tile, width), returned.dtype),
+        out_shape=(
+            jax.ShapeDtypeStruct((tiles_here, tile, width), returned.dtype),
+            jax.ShapeDtypeStruct(grad_emb.shape, grad_emb.dtype),
+        ),
         grid_spec=pltpu.PrefetchScalarGridSpec(
             num_scalar_prefetch=3,
-            grid=(tiles_here // per_step,),
-            in_specs=[pl.BlockSpec(memory_space=pltpu.VMEM)],
-            out_specs=pl.BlockSpec((per_step, tile, width), lambda i, *refs: (i, 0, 0)),
+            grid=(steps,),
+            in_specs=[pl.BlockSpec(memory_space=pltpu.VMEM), emb_spec],
+            out_specs=(
+                pl.BlockSpec((per_step, tile, width), lambda i, *refs: (i, 0, 0)),
+                emb_spec,
+            ),
             scratch_shapes=[pltpu.VMEM((tile, width), jnp.float32)],
         ),
         compiler_params=pltpu.CompilerParams(vmem_limit_bytes=24 * 2**20),
-    )(pick, uses, first, returned)
+    )(pick, uses, first, returned, grad_emb)
 
 
 def main_kernel(
@@ -202,7 +212,8 @@
     grad_emb,
     returned,
     loss_out,
-    incoming,
+    incoming_a,
+    incoming_b,
     tiles,
     scores,
     partial,
@@ -236,6 +247,8 @@
     cols = list_len * TILE
     half = rows // 2
     chunks = half // CHUNK
+    part_cols = cols // 2
+    incoming = (incoming_a, incoming_b)
     last = dp_count - 1
 
     barrier = pltpu.get_barrier_semaphore()
@@ -249,52 +262,54 @@
         )
     pl.semaphore_wait(barrier, groups + dp_count - 2)
 
-    def tile_copy(k):
+    def tile_copy(h, k):
         to = lax.rem(me + k, groups)
         return pltpu.make_async_remote_copy(
-            src_ref=out_tiles.at[pl.ds(to * CAP, CAP)],
-            dst_ref=incoming.at[pl.ds(me * CAP, CAP)],
-            send_sem=tile_send.at[k],
-            recv_sem=tile_recv.at[k],
+            src_ref=out_tiles.at[pl.ds(to * CAP, CAP), pl.ds(h * HALF, HALF)],
+            dst_ref=incoming[h].at[pl.ds(me * CAP, CAP)],
+            send_sem=tile_send.at[h, k],
+            recv_sem=tile_recv.at[h, k],
             device_id={"proto": to},
             device_id_type=MESH,
         )
 
-    for k in range(1, groups):
-        tile_copy(k).start()
-    own = pltpu.make_async_copy(
-        out_tiles.at[pl.ds(me * CAP, CAP)], incoming.at[pl.ds(me * CAP, CAP)], own_sem
-    )
-    own.start()
+    def own_copy(h):
+        return pltpu.make_async_copy(
+            out_tiles.at[pl.ds(me * CAP, CAP), pl.ds(h * HALF, HALF)],
+            incoming[h].at[pl.ds(me * CAP, CAP)],
+            own_sem.at[h],
+        )
+
+    def tiles_in(h):
+        own_copy(h).wait()
+        for k in range(1, groups):
+            tile_copy(h, k).wait()
+        for j in range(list_len):
+            at = h * part_cols + j * HALF
+            tiles[at : at + HALF, :] = incoming[h][slot_ref[j]]
+
+    for h in range(2):
+        for k in range(1, groups):
+            tile_copy(h, k).start()
+        own_copy(h).start()
     loss_acc[...] = jnp.zeros_like(loss_acc)
-    own.wait()
-    for k in range(1, groups):
-        tile_copy(k).wait()
-    for j in range(list_len):
-        tiles[j * TILE : (j + 1) * TILE, :] = incoming[slot_ref[j]]
+    tiles_in(0)
 
     block = min(256, half)
-
-    def score_block(i, carry):
-        at = pl.ds(pl.multiple_of(i * block, block), block)
-        scores[at, :] = lax.dot_general(
-            emb[at, :], tiles[...], (((1,), (1,)), ((), ())), preferred_element_type=jnp.float32
-        )
-        return carry
-
-    lax.fori_loop(0, rows // block, score_block, 0)
+    group = 128 // CHUNK
 
     def rows_of(way, c):
         return pl.multiple_of((1 - way) * half + c * CHUNK, CHUNK)
 
-    def part_copy(way, c, first):
-        dst = partial.at[way, pl.ds(pl.multiple_of(c * CHUNK, CHUNK), CHUNK)]
-        src = scores.at[pl.ds(rows_of(way, c), CHUNK)] if first else dst
+    def part_copy(way, h, c, first):
+        lanes = pl.ds(pl.multiple_of(h * part_cols, part_cols), part_cols)
+        dst = partial.at[way, pl.ds(pl.multiple_of(c * CHUNK, CHUNK), CHUNK), lanes]
+        src = scores.at[pl.ds(rows_of(way, c), CHUNK), lanes] if first else dst
         return pltpu.make_async_remote_copy(
             src_ref=src,
             dst_ref=dst,
-            send_sem=part_send.at[way, c],
-            recv_sem=part_recv.at[way, c],
+            send_sem=part_send.at[way, h, c],
+            recv_sem=part_recv.at[way, h, c],
             device_id={"dp": jnp.clip(z + 1 - 2 * way, 0, last)},
             device_id_type=MESH,
         )
@@ -316,26 +331,41 @@
         way = lax.rem(i, 2)
         s = i // 2
         pos = jnp.where(way == 0, z, last - z)
-        c = s - LAG * pos
-
-        @pl.when((c >= 0) & (c < chunks))
+        turn = s - LAG * pos
+
+        @pl.when((turn >= 0) & (turn < 2 * chunks))
         def _():
+            h = turn // chunks
+            c = lax.rem(turn, chunks)
+            lanes = pl.ds(pl.multiple_of(h * part_cols, part_cols), part_cols)
+
+            @pl.when(lax.rem(c, group) == 0)
+            def _():
+                these = pl.ds(rows_of(way, c), group * CHUNK)
+                scores[these, lanes] = lax.dot_general(
+                    emb[these, :],
+                    tiles[lanes, :],
+                    (((1,), (1,)), ((), ())),
+                    preferred_element_type=jnp.float32,
+                )
+
             at = pl.ds(rows_of(way, c), CHUNK)
             here = pl.ds(pl.multiple_of(c * CHUNK, CHUNK), CHUNK)
 
             @pl.when(pos == 0)
             def _():
-                part_copy(way, c, True).start()
+                part_copy(way, h, c, True).start()
 
             @pl.when((pos > 0) & (pos < last))
             def _():
-                part_copy(way, c, False).wait_recv()
-                partial[way, here, :] += scores[at, :]
-                part_copy(way, c, False).start()
-
-            @pl.when(pos == last)
+                part_copy(way, h, c, False).wait_recv()
+                partial[way, here, lanes] += scores[at, lanes]
+                part_copy(way, h, c, False).start()
+
+            @pl.when((pos == last) & (h == 1))
             def _():
-                part_copy(way, c, False).wait_recv()
+                part_copy(way, 0, c, False).wait_recv()
+                part_copy(way, 1, c, False).wait_recv()
                 score = (partial[way, here, :] + scores[at, :]) * inv_scale
                 onehot = lane == column[at, :]
                 top = jnp.max(score, axis=1, keepdims=True)
@@ -346,7 +376,7 @@
                 dz[at, :] = (expo / total - jnp.where(onehot, 1.0, 0.0)).astype(dz.dtype)
                 dz_copy(way, c).start()
 
-        c2 = s - LAG * last - LAG * (last - pos)
+        c2 = s - chunks - LAG * last - LAG * (last - pos)
 
         @pl.when((c2 >= 0) & (c2 < chunks) & (pos < last))
         def _():
@@ -358,7 +388,9 @@
 
         return carry
 
-    lax.fori_loop(0, 2 * (chunks + 2 * LAG * last), step, 0)
+    lax.fori_loop(0, 2 * chunks, step, 0)
+    tiles_in(1)
+    lax.fori_loop(2 * chunks, 2 * (2 * chunks + 2 * LAG * last), step, 0)
 
     loss_mine[...] = jnp.broadcast_to(jnp.sum(loss_acc[...], axis=0, keepdims=True), (8, 128))
 
@@ -383,8 +415,9 @@
             (((0,), (0,)), ((), ())),
             preferred_element_type=jnp.float32,
         ).astype(piece.dtype)
-        for t in range(wide // TILE):
-            piece[j * (wide // TILE) + t] = out[t * TILE : (t + 1) * TILE, :]
+        for t in range(wide // HALF):
+            h, tile = divmod(j * (wide // HALF) + t, list_len)
+            piece[tile, h * HALF : (h + 1) * HALF, :] = out[t * HALF : (t + 1) * HALF, :]
 
     def ret_copy(k):
         to = lax.rem(me + k, groups)
@@ -453,7 +486,8 @@
 
         @pl.when(pos < last)
         def _():
-            part_copy(way, c, False).wait_send()
+            part_copy(way, 0, c, False).wait_send()
+            part_copy(way, 1, c, False).wait_send()
 
         @pl.when(pos > 0)
         def _():
@@ -493,7 +527,12 @@
         axis=1,
     )
     hit = (my_ids[None, :] == (labels // TILE)[:, None]).astype(jnp.int32)
-    column = (jnp.sum(hit * (order * TILE)[None, :], axis=1) + labels % TILE)[:, None]
+    within = labels % TILE
+    column = (
+        jnp.sum(hit * (order * HALF)[None, :], axis=1)
+        + within // HALF * (cols // 2)
+        + within % HALF
+    )[:, None]
     outgoing = pack_tiles(table.reshape(tiles_here, TILE, width), select)
     chunks = block_rows // 2 // CHUNK
     bf16, f32 = jnp.bfloat16, jnp.float32
@@ -511,7 +550,8 @@
         in_specs=[smem, smem, hbm, vmem, vmem],
         out_specs=(vmem, hbm, vmem),
         scratch_shapes=[
-            pltpu.VMEM((slots, TILE, width), bf16),
+            pltpu.VMEM((slots, HALF, width), bf16),
+            pltpu.VMEM((slots, HALF, width), bf16),
             pltpu.VMEM((cols, width), bf16),
             pltpu.VMEM((block_rows, cols), f32),
             pltpu.VMEM((2, block_rows // 2, cols), f32),
@@ -523,11 +563,11 @@
             pltpu.VMEM((groups, 8, 128), f32),
             pltpu.VMEM((8, 128), f32),
             pltpu.VMEM((dp_count, 8, 128), f32),
-            dma((groups,)),
-            dma((groups,)),
-            dma,
-            dma((2, chunks)),
-            dma((2, chunks)),
+            dma((2, groups)),
+            dma((2, groups)),
+            dma((2,)),
+            dma((2, 2, chunks)),
+            dma((2, 2, chunks)),
             dma((2, chunks)),
             dma((2, chunks)),
             dma((groups,)),
@@ -542,7 +582,9 @@
             collective_id=0, has_side_effects=True, vmem_limit_bytes=VMEM_LIMIT
         ),
     )(my_slot, back, outgoing, embeddings, column)
-    grad_table = place_tiles(returned, jnp.where(taken, select, -1), tiles_here)
+    grad_table, grad_emb = place_tiles(
+        returned, jnp.where(taken, select, -1), grad_emb, tiles_here
+    )
     return (loss[0, 0] / total_rows, grad_emb, grad_table.reshape(tiles_here * TILE, width))
 
 

time: 179 us -> 164 us (0.916); the launches traced: 177 us -> 164 us
  Pallas kernels: 160 us -> 147 us
    pallas_call x1, Pallas kernels: 152 us -> 137 us  [fused_body(): pl.pallas_call(functools.partial(main_kernel, groups, dp_count, 1.0 / mat...]
    unnamed x11 -> x10, local copies, waits for them, and re-layouts: 6.77 us -> 7.03 us
where the time goes in v3:
time: 164 us
  Pallas kernels  147 us (90%)
  local copies, waits for them, and re-layouts  10.3 us (6%)
  other arithmetic  4.2 us (3%)
  between operations  2.5 us (2%)
    pallas_call x1, Pallas kernels, fused_body(): pl.pallas_call(functools.partial(main_kernel, groups, dp_count, 1.0 / mat...  137 us
    unnamed x10, local copies, waits for them, and re-layouts  7.03 us
    pallas_call x1, Pallas kernels, place_tiles(): pl.pallas_call(functools.partial(place_kernel, per_step, count), out_shap...  5.45 us
    pallas_call x1, Pallas kernels, pack_tiles(): pl.pallas_call(pack_kernel, out_shape=jax.ShapeDtypeStruct((count, tile,...  4.14 us

profile of v3, /device:TPU:0, one launch (start us, length us, event | category | flops | bytes accessed | tf_op | source)
XLA Modules:
  0.0 164.0 jit_solution(12263038608385144567)
XLA Ops:
  0.6 0.7 dynamic-slice_bitcast_fusion
  1.3 0.7 add_select_fusion.3
  2.0 0.1 select_reduce_fusion
  2.1 0.7 fusion.4
  2.8 0.7 add_select_fusion.4
  3.5 0.7 broadcast_compare_fusion
  4.2 0.3 convert_reduce_fusion
  4.5 0.2 select_reduce_fusion.2
  4.7 0.2 fusion.1
  4.8 0.0 copy-start.4
  4.9 0.6 select_reduce_fusion.3.back_ref
  5.5 0.1 copy.10
  5.6 0.1 reshape.53
  5.7 0.1 copy.8
  5.7 0.1 reshape.51.pick_ref
  5.8 0.1 select_reduce_fusion.1
  5.9 1.0 copy.9.column
  7.0 0.0 copy-start.1
  7.0 2.5 %copy-done.1 = bf16[4096,640]{1,0:T(8,128)(2,1)S(1)} copy-done((bf16[4096,640]{1,0:T(8,128)(2,1)S(1)}, bf16[4096,640]{1,0:T(8,128)(2,1)}, u32[]{:S(2)}) %copy-start.1) | copy-done | bytes 5242904
  9.4 4.1 %shard_map.67.out_tiles = bf16[16,128,640]{2,1,0:T(8,128)(2,1)S(1)} custom-call(s32[16]{0:T(128)S(1)} %reshape.51.pick_ref, bf16[32,128,640]{2,1,0:T(8,128)(2,1)S(1)} %bitcast.8), custom_call_target="tpu_custom_call" | custom-call | tf_op jit(solution)/shard_map/pallas_call | solution.py:131
  13.6 0.0 copy-done.4
  13.6 0.0 copy-start
  13.6 1.5 copy-done
  15.1 137.5 %shard_map.68 = (bf16[1024,640]{1,0:T(8,128)(2,1)}, bf16[16,128,640]{2,1,0:T(8,128)(2,1)}, f32[8,128]{1,0:T(8,128)}) custom-call(s32[8]{0:T(128)} %copy-done.4, s32[16]{0:T(128)} %select_reduce_fusion.3.back_ref, bf16[16,128,640]{2,1,0:T(8,128)(2,1)} %copy-done, bf16[1024,640]{1,0:T(8,128)(2,1)} %emb.1, s32[1024,1]{1,0:T(8,128)} %copy.9.column), custom_call_target="tpu_custom_call" | custom-call | tf_op jit(solution)/shard_map/pallas_call | solution.py:543
  152.6 1.2 slice.3
  154.4 0.0 copy-start.2
  154.4 1.7 %copy-done.2 = bf16[16,128,640]{2,1,0:T(8,128)(2,1)S(1)} copy-done((bf16[16,128,640]{2,1,0:T(8,128)(2,1)S(1)}, bf16[16,128,640]{2,1,0:T(8,128)(2,1)}, u32[]{:S(2)}) %copy-start.2) | copy-done | bytes 2621464
  156.1 0.0 copy-start.3
  156.1 1.3 copy-done.3
  157.5 5.4 %shard_map.69 = (bf16[32,128,640]{2,1,0:T(8,128)(2,1)}, bf16[1024,640]{1,0:T(8,128)(2,1)}) custom-call(s32[16]{0:T(128)S(1)} %broadcast_select_fusion.pick_ref, s32[32]{0:T(128)S(1)} %get-tuple-element.14.uses_ref, s32[32]{0:T(128)S(1)} %get-tuple-element.13.first_ref, bf16[16,128,640]{2,1,0:T(8,128)(2,1)S(1)} %copy-done.2, bf16[1024,640]{1,0:T(8,128)(2,1)S(1)} %copy-done.3), custom_call_target="tpu_custom_call" | custom-call | tf_op jit(solution)/shard_map/pallas_call | solution.py:183
  (4 shorter events, 0.0 us)
Async XLA Ops:
  4.8 8.8 %copy-start.4 = (s32[8]{0:T(128)}, s32[8]{0:T(128)S(1)}, u32[]{:S(2)}) copy-start(s32[8]{0:T(128)S(1)} %dynamic-slice_bitcast_fusion.1.slot_ref) | copy-start | bytes 100
  7.0 2.5 %copy-start.1 = (bf16[4096,640]{1,0:T(8,128)(2,1)S(1)}, bf16[4096,640]{1,0:T(8,128)(2,1)}, u32[]{:S(2)}) copy-start(bf16[4096,640]{1,0:T(8,128)(2,1)} %param.5) | copy-start | bytes 15728644
  13.6 1.5 copy-start
  154.4 1.7 %copy-start.2 = (bf16[16,128,640]{2,1,0:T(8,128)(2,1)S(1)}, bf16[16,128,640]{2,1,0:T(8,128)(2,1)}, u32[]{:S(2)}) copy-start(bf16[16,128,640]{2,1,0:T(8,128)(2,1)} %get-tuple-element.9.got_ref) | copy-start | bytes 7864324
  156.1 1.3 copy-start.3

commit v4 on v3

--- a/solution.py
+++ b/solution.py
@@ -196,7 +196,7 @@
             ),
             scratch_shapes=[pltpu.VMEM((tile, width), jnp.float32)],
         ),
-        compiler_params=pltpu.CompilerParams(vmem_limit_bytes=24 * 2**20),
+        compiler_params=pltpu.CompilerParams(vmem_limit_bytes=VMEM_LIMIT),
     )(pick, uses, first, returned, grad_emb)
 
 
@@ -407,34 +407,37 @@
     for k in range(1, groups):
         lp_copy(k).start()
 
-    wide = min(256, cols)
-    for j in range(cols // wide):
-        out = lax.dot_general(
-            dz[:, j * wide : (j + 1) * wide],
-            emb[...],
-            (((0,), (0,)), ((), ())),
-            preferred_element_type=jnp.float32,
-        ).astype(piece.dtype)
-        for t in range(wide // HALF):
-            h, tile = divmod(j * (wide // HALF) + t, list_len)
-            piece[tile, h * HALF : (h + 1) * HALF, :] = out[t * HALF : (t + 1) * HALF, :]
-
-    def ret_copy(k):
+    wide = min(256, part_cols)
+
+    def ret_copy(h, k):
         to = lax.rem(me + k, groups)
+        these = pl.ds(h * HALF, HALF)
         return pltpu.make_async_remote_copy(
-            src_ref=ret.at[pl.ds(to * CAP, CAP)],
-            dst_ref=returned.at[pl.ds(me * CAP, CAP)],
-            send_sem=ret_send.at[k],
-            recv_sem=ret_recv.at[k],
+            src_ref=ret.at[pl.ds(to * CAP, CAP), these],
+            dst_ref=returned.at[pl.ds(me * CAP, CAP), these],
+            send_sem=ret_send.at[h, k],
+            recv_sem=ret_recv.at[h, k],
             device_id={"proto": to},
             device_id_type=MESH,
         )
 
-    for k in range(1, groups):
-        to = lax.rem(me + k, groups)
-        for t in range(CAP):
-            ret[to * CAP + t] = piece[back_ref[to * CAP + t]]
-        ret_copy(k).start()
+    for h in range(2):
+        these = slice(h * HALF, (h + 1) * HALF)
+        for j in range(part_cols // wide):
+            at = h * part_cols + j * wide
+            out = lax.dot_general(
+                dz[:, at : at + wide],
+                emb[...],
+                (((0,), (0,)), ((), ())),
+                preferred_element_type=jnp.float32,
+            ).astype(piece.dtype)
+            for t in range(wide // HALF):
+                piece[j * (wide // HALF) + t, these, :] = out[t * HALF : (t + 1) * HALF, :]
+        for k in range(1, groups):
+            to = lax.rem(me + k, groups)
+            for t in range(CAP):
+                ret[to * CAP + t, these, :] = piece[back_ref[to * CAP + t], these, :]
+            ret_copy(h, k).start()
     for t in range(CAP):
         ret[me * CAP + t] = piece[back_ref[me * CAP + t]]
     own_ret = pltpu.make_async_copy(
@@ -497,8 +500,9 @@
 
     lax.fori_loop(0, 2 * chunks, drain, 0)
     own_ret.wait()
-    for k in range(1, groups):
-        ret_copy(k).wait()
+    for h in range(2):
+        for k in range(1, groups):
+            ret_copy(h, k).wait()
 
 
 def fused_body(embeddings, table, tile_lists, labels):
@@ -570,8 +574,8 @@
             dma((2, 2, chunks)),
             dma((2, chunks)),
             dma((2, chunks)),
-            dma((groups,)),
-            dma((groups,)),
+            dma((2, groups)),
+            dma((2, groups)),
             dma,
             dma((groups,)),
             dma((groups,)),

time: 164 us -> 164 us (level)
  local copies, waits for them, and re-layouts: 10.3 us -> 7.24 us
  Pallas kernels: 147 us -> 149 us
    unnamed x10 -> x8, local copies, waits for them, and re-layouts: 7.03 us -> 3.98 us
    pallas_call x1, Pallas kernels: 5.45 us -> 8.16 us  [place_tiles(): pl.pallas_call(functools.partial(place_kernel, per_step, count), out_shap...]
where the time goes in v4:
time: 164 us
  Pallas kernels  149 us (91%)
  local copies, waits for them, and re-layouts  7.24 us (4%)
  other arithmetic  4.71 us (3%)
  between operations  2.5 us (2%)
    pallas_call x1, Pallas kernels, fused_body(): pl.pallas_call(functools.partial(main_kernel, groups, dp_count, 1.0 / mat...  137 us
    pallas_call x1, Pallas kernels, place_tiles(): pl.pallas_call(functools.partial(place_kernel, per_step, count), out_shap...  8.16 us
    pallas_call x1, Pallas kernels, pack_tiles(): pl.pallas_call(pack_kernel, out_shape=jax.ShapeDtypeStruct((count, tile,...  4.14 us
    unnamed x8, local copies, waits for them, and re-layouts  3.98 us

profile of v4, /device:TPU:0, one launch (start us, length us, event | category | flops | bytes accessed | tf_op | source)
XLA Modules:
  0.0 163.6 jit_solution(894047167160337787)
XLA Ops:
  0.6 0.7 dynamic-slice_bitcast_fusion
  1.3 0.7 add_select_fusion.3
  2.0 0.1 select_reduce_fusion
  2.1 0.7 fusion.4
  2.8 0.7 add_select_fusion.4
  3.5 0.7 broadcast_compare_fusion
  4.2 0.3 convert_reduce_fusion
  4.5 0.2 select_reduce_fusion.2
  4.7 0.2 fusion.1
  4.8 0.0 copy-start.3
  4.9 0.6 select_reduce_fusion.3.back_ref
  5.4 0.1 copy.10
  5.5 0.1 reshape.53
  5.6 0.1 copy.8
  5.7 0.1 reshape.51.pick_ref
  5.8 0.0 copy-start.2
  5.8 0.6 select_reduce_fusion.1
  6.4 1.0 copy.9.column
  7.5 0.0 copy-start.1
  7.5 2.5 %copy-done.1 = bf16[4096,640]{1,0:T(8,128)(2,1)S(1)} copy-done((bf16[4096,640]{1,0:T(8,128)(2,1)S(1)}, bf16[4096,640]{1,0:T(8,128)(2,1)}, u32[]{:S(2)}) %copy-start.1) | copy-done | bytes 5242904
  10.0 4.1 %shard_map.67.out_tiles = bf16[16,128,640]{2,1,0:T(8,128)(2,1)S(1)} custom-call(s32[16]{0:T(128)S(1)} %reshape.51.pick_ref, bf16[32,128,640]{2,1,0:T(8,128)(2,1)S(1)} %bitcast.8), custom_call_target="tpu_custom_call" | custom-call | tf_op jit(solution)/shard_map/pallas_call | solution.py:131
  14.1 0.0 copy-done.3
  14.1 0.0 copy-done.2
  14.1 0.0 copy-start
  14.1 1.5 copy-done
  15.6 136.8 %shard_map.68 = (bf16[1024,640]{1,0:T(8,128)(2,1)}, bf16[16,128,640]{2,1,0:T(8,128)(2,1)}, f32[8,128]{1,0:T(8,128)}) custom-call(s32[8]{0:T(128)} %copy-done.3, s32[16]{0:T(128)} %select_reduce_fusion.3.back_ref, bf16[16,128,640]{2,1,0:T(8,128)(2,1)} %copy-done, bf16[1024,640]{1,0:T(8,128)(2,1)} %emb.1, s32[1024,1]{1,0:T(8,128)} %copy.9.column), custom_call_target="tpu_custom_call" | custom-call | tf_op jit(solution)/shard_map/pallas_call | solution.py:547
  152.4 1.2 slice.3
  154.3 8.2 %shard_map.69 = (bf16[32,128,640]{2,1,0:T(8,128)(2,1)}, bf16[1024,640]{1,0:T(8,128)(2,1)}) custom-call(s32[16]{0:T(128)} %copy-done.2, s32[32]{0:T(128)} %get-tuple-element.14.uses_ref, s32[32]{0:T(128)} %get-tuple-element.13.first_ref, bf16[16,128,640]{2,1,0:T(8,128)(2,1)} %get-tuple-element.9.got_ref, bf16[1024,640]{1,0:T(8,128)(2,1)} %get-tuple-element.10.emb_in), custom_call_target="tpu_custom_call" | custom-call | tf_op jit(solution)/shard_map/pallas_call | solution.py:183
  (4 shorter events, 0.0 us)
Async XLA Ops:
  4.8 9.3 %copy-start.3 = (s32[8]{0:T(128)}, s32[8]{0:T(128)S(1)}, u32[]{:S(2)}) copy-start(s32[8]{0:T(128)S(1)} %dynamic-slice_bitcast_fusion.1.slot_ref) | copy-start | bytes 100
  5.8 8.3 %copy-start.2 = (s32[16]{0:T(128)}, s32[16]{0:T(128)S(1)}, u32[]{:S(2)}) copy-start(s32[16]{0:T(128)S(1)} %broadcast_select_fusion.pick_ref) | copy-start | bytes 196
  7.5 2.5 %copy-start.1 = (bf16[4096,640]{1,0:T(8,128)(2,1)S(1)}, bf16[4096,640]{1,0:T(8,128)(2,1)}, u32[]{:S(2)}) copy-start(bf16[4096,640]{1,0:T(8,128)(2,1)} %param.5) | copy-start | bytes 15728644
  14.1 1.5 copy-start
